TPU v7x, 32 devices: a whole 2x2x4 slice. The times are simulated.
32 devices in a mesh: tm: 2 (over x), pair: 16 (over z, y, core).
Axes of the slice: x: 2, y: 2, z: 4, core: 2. Of those that a mesh axis runs over, the one named last changes fastest.
Arguments:
- traces: float32 [4, 2048, 1024], P('tm', 'pair'), may hold values from -6 to 6
- owner: int32 [16], replicated, may hold values from 0 to 15, each once
- tiles: int32 [48, 2], P('pair'), may hold values from 0 to 15, as said below
- counts: int32 [16], P('pair'), may hold values from 1 to 3, as said below
Outputs:
- stacks: float32 [48, 128, 16384], P('pair', None, 'tm')
Inputs may be any that keep to these rules, and one draw needn't show every extreme that they name: `tiles`: each row names fiber blocks a <= b with b - a at most 6. `counts`: the first that many of an index's 3 slots are live; some index has all 3 live.
All inputs are finite; a program needn't handle non-finite values.
Results may differ from a plain program's by a relative error of at most 0.0038.
Values may be sent and summed in bfloat16 or wider, within the bound.
No kernel may reach another device: no remote copies, remote signals or barrier semaphores. Data moves between devices by JAX's collectives and lax.ppermute only.
A program may use at most 128 MiB of HBM per device.

v0:
```python
import functools
import math

import jax
import jax.numpy as jnp
import numpy as np
from jax import lax
from jax.experimental import pallas as pl
from jax.experimental.pallas import tpu as pltpu
from jax.sharding import PartitionSpec as P

NT = 1024
NF = 128
LOW_BIN = 8
LAGS = 128


def forward_table():
    phase = (LOW_BIN + np.arange(NF))[:, None] * np.arange(NT)[None, :] % NT
    angle = phase * (2.0 * math.pi / NT)
    return np.concatenate([np.cos(angle), -np.sin(angle)], axis=0).astype(np.float32)


def inverse_table(segments, sent):
    (shifts,) = after([jnp.arange(LAGS, dtype=jnp.int32) - LAGS // 2], sent)
    column = jnp.arange(2 * NF, dtype=jnp.int32)
    half = NF // PIECES
    bin_id = LOW_BIN + column // (2 * half) * half + column % half
    phase = jnp.mod(shifts[:, None] * bin_id[None, :], NT)
    angle = phase.astype(jnp.float32) * (2.0 * math.pi / NT)
    scale = 1.0 / math.sqrt(segments * NF)
    value = jnp.where(column // half % 2 == 0, jnp.cos(angle), -jnp.sin(angle)) * scale
    return value.astype(jnp.bfloat16)


def halves(value):
    high = value.astype(jnp.bfloat16)
    return high, (value - high.astype(jnp.float32)).astype(jnp.bfloat16)


def nt_dot(a, b):
    return lax.dot_general(a, b, (((1,), (1,)), ((), ())), preferred_element_type=jnp.float32)


CHUNKS = 2
PIECES = 2


def whiten_kernel(bins, x_hbm, table_hbm, *refs):
    outs, (x_ref, table_ref, pad_ref, sems) = refs[:-4], refs[-4:]
    _, segments, block, wide = x_ref.shape
    columns = segments * block
    copies = []
    for k in range(CHUNKS):
        span = slice(k * wide, (k + 1) * wide)
        sources = (x_hbm.at[:, :, span], table_hbm.at[:, span])
        copies.append(
            [
                pltpu.make_async_copy(source, target.at[k], sems.at[k, n])
                for n, (source, target) in enumerate(zip(sources, (x_ref, table_ref)))
            ]
        )
        for copy in copies[-1]:
            copy.start()
    spectrum = None
    for k in range(CHUNKS):
        for copy in copies[k]:
            copy.wait()
        x = x_ref[k].reshape(columns, wide)
        x_high, x_low = halves(x)
        high, low = halves(table_ref[k])
        part = nt_dot(high, x_high) + nt_dot(high, x_low) + nt_dot(low, x_high)
        spectrum = part if spectrum is None else spectrum + part
    real_part = spectrum[:NF]
    imag_part = spectrum[NF:]
    power = real_part * real_part + imag_part * imag_part
    edge = jnp.zeros((8, columns), jnp.float32)
    pad_ref[0:8, :] = edge
    pad_ref[8 + NF : 16 + NF, :] = edge
    pad_ref[8 : 8 + NF, :] = power
    total = pad_ref[6 : 6 + NF, :]
    for offset in range(7, 11):
        total = total + pad_ref[offset : offset + NF, :]
    bin_id = lax.broadcasted_iota(jnp.int32, (NF, columns), 0)
    counted = (jnp.minimum(bin_id + 2, NF - 1) - jnp.maximum(bin_id - 2, 0) + 1).astype(jnp.float32)
    smooth = total / counted
    level = jnp.mean(power, axis=0, keepdims=True)
    factor = lax.rsqrt(smooth + 0.05 * level + 1e-06)
    parts = ((real_part * factor).astype(jnp.bfloat16), (imag_part * factor).astype(jnp.bfloat16))
    each = NF // bins // len(outs)
    for group in range(NF // bins):
        for segment in range(segments):
            for c in range(2):
                row = ((group % each * segments + segment) * 2 + c) * bins
                outs[group // each][row : row + bins, :] = parts[c][
                    group * bins : (group + 1) * bins, segment * block : (segment + 1) * block
                ]


def fetch(joined, plan_ref, at, wanted, sources, targets):
    index = plan_ref[wanted + at]
    for n, source in enumerate(sources):

        @pl.when(plan_ref[at] == n)
        def _():
            for step in range(joined):
                value = source[index + step]
                for target in targets[step]:
                    target[...] = value


def pick_kernel(count, plan_ref, *refs):
    sources, outs, (held, turned) = refs[:count], refs[count:-2], refs[-2:]
    slots, rows, block = held.shape
    times = len(outs)
    share = block // times
    time = plan_ref[4 * slots]
    for slot in range(slots):
        fetch(1, plan_ref, 2 * slot, 2 * slots, sources, [[held.at[slot]]])
        fetch(1, plan_ref, 2 * slot + 1, 2 * slots, sources, [[out.at[slot, :rows] for out in outs]])
    for slot in range(slots):
        flipped = held[slot].astype(jnp.float32).T.astype(jnp.bfloat16)
        for piece in range(rows // block):
            turned[slot, piece] = flipped[:, piece * block : (piece + 1) * block]
        for step, out in enumerate(outs):
            start = pl.multiple_of((time + step) % times * share, share)
            for piece in range(rows // block):
                low = rows + piece * share
                out[slot, low : low + share] = turned[slot, piece, pl.ds(start, share)]


def put_right(bins, block_ref, right_all, at, rows):
    block = block_ref.shape[1]
    for low in range(0, rows, 2 * bins):
        real_part = block_ref[low : low + bins, :]
        imag_part = block_ref[low + bins : low + 2 * bins, :]
        base = at(low)
        right_all[base : base + bins, :block] = real_part
        right_all[base : base + bins, block:] = imag_part
        right_all[base + bins : base + 2 * bins, :block] = imag_part
        right_all[base + bins : base + 2 * bins, block:] = -real_part


def put_pack(slot, rows, bins, step, times, pack, left_all, right_all):
    share = left_all.shape[0]
    block = share * times
    wide = times * rows
    part_rows = left_all.shape[1] // times
    at = functools.partial(column_of, rows, wide, step)
    put_right(bins, pack.at[slot], right_all, at, part_rows)
    for low in range(0, part_rows, block):
        first = part_rows + low // block * share
        value = pack[slot, first : first + share, :].astype(jnp.float32)
        for inner in range(0, block, rows):
            left_all[:, at(low + inner) : at(low + inner) + rows] = value[:, inner : inner + rows]


def column_of(rows, wide, step, low):
    return low // rows * wide + step * rows + low % rows


def cross_spectra(bins, wide, first, chunk, left_all, right_all, cross_ref):
    groups = left_all.shape[1] // wide
    block = right_all.shape[1] // 2
    half = groups * bins
    column = lax.broadcasted_iota(jnp.int32, (bins, wide), 1) % bins
    row = lax.broadcasted_iota(jnp.int32, (bins, wide), 0)
    keep = (column == row).astype(jnp.float32).astype(jnp.bfloat16)
    several = 16 if chunk % 16 == 0 else 2
    for group in range(groups):
        weights = right_all[group * wide : (group + 1) * wide, :]
        for start in range(0, chunk, several):
            pieces = []
            for i in range(several):
                line = left_all[pl.ds(first + start + i, 1), group * wide : (group + 1) * wide]
                tile = jnp.broadcast_to(line, (16, wide)).astype(jnp.bfloat16)
                pieces += [tile * keep[low : low + 16] for low in range(0, bins, 16)]
            product = jnp.dot(jnp.concatenate(pieces, axis=0), weights, preferred_element_type=jnp.float32)
            product = product.astype(jnp.bfloat16)
            for i in range(several):
                at = start + i
                lanes = slice(at % 2 * block, (at % 2 + 1) * block)
                piece = product[i * bins : (i + 1) * bins]
                cross_ref[at // 2, group * bins : (group + 1) * bins, lanes] = piece[:, :block]
                cross_ref[at // 2, half + group * bins : half + (group + 1) * bins, lanes] = piece[:, block:]


def cross_kernel(bins, rows, chunk, plan_ref, *refs):
    packs, (out_ref, left_all, right_all) = refs[:-3], refs[-3:]
    times = len(packs)

    def one_slot(slot, carry):
        for step, pack in enumerate(packs):
            put_pack(slot, rows, bins, step, times, pack, left_all, right_all)
        for n in range(left_all.shape[0] // chunk):
            into = out_ref.at[slot, n * chunk // 2 : (n + 1) * chunk // 2]
            cross_spectra(bins, times * rows, n * chunk, chunk, left_all, right_all, into)
        return carry

    slots = out_ref.shape[0]
    lax.fori_loop(0, jnp.minimum(plan_ref[4 * slots + 1], slots), one_slot, 0)


def stack_kernel(bins, rows, times, chunk, joined, plan_ref, table_ref, early_ref, *refs):
    sources, refs = refs[:-8], refs[-8:]
    out_ref, held, blocks, turned, left_all, right_all, cross_ref, sems = refs
    slots = held.shape[0]
    live = plan_ref[4 * slots + 1]
    share = left_all.shape[0]
    block = share * times
    wide = times * rows
    part_rows = left_all.shape[1] // times
    lanes = 2 * block
    parts = share // chunk
    width = chunk // 2 * lanes

    def leave(slot, n):
        span = slice(n * width, (n + 1) * width)
        return pltpu.make_async_copy(held.at[slot, :, span], out_ref.at[slot, :, span], sems.at[slot, n])

    def one_slot(slot, carry):
        if joined == 1:
            for step, pack in enumerate(sources):
                put_pack(slot, rows, bins, step, times, pack, left_all, right_all)
        else:
            for side in range(2):
                targets = [[blocks.at[side, step]] for step in range(joined)]
                fetch(joined, plan_ref, 2 * slot + side, 2 * slots, sources, targets)
            start = pl.multiple_of(plan_ref[4 * slots] * share, share)
            for step in range(times):
                at = functools.partial(column_of, rows, wide, step)
                put_right(bins, blocks.at[1, step], right_all, at, part_rows)
                turned[...] = blocks[0, step].astype(jnp.float32).T
                for low in range(0, part_rows, rows):
                    left_all[:, at(low) : at(low) + rows] = turned[pl.ds(start, share), low : low + rows]
        table = table_ref[...]
        for n in range(parts):
            cross_spectra(bins, wide, n * chunk, chunk, left_all, right_all, cross_ref.at[n % 2])
            for pair in range(chunk // 2):
                at = n * chunk // 2 + pair
                cross = jnp.concatenate([early_ref[slot, at], cross_ref[n % 2, pair]], axis=0)
                held[slot, :, at * lanes : (at + 1) * lanes] = jnp.dot(table, cross, preferred_element_type=jnp.float32)
            leave(slot, n).start()
        return carry

    for slot in range(slots):

        @pl.when(slot >= live)
        def _():
            held[slot] = jnp.zeros_like(held[slot])
            for n in range(parts):
                leave(slot, n).start()

    lax.fori_loop(0, jnp.minimum(live, slots), one_slot, 0)
    for slot in range(slots):
        for n in range(parts):
            leave(slot, n).wait()


def chip_dims(size):
    return {16: (4, 2, 2), 64: (16, 4, 1)}.get(size, (size, 1, 1))


def swap(value, dims, axis, by):
    moves = []
    for p in range(math.prod(dims)):
        place = list(np.unravel_index(p, dims))
        place[axis] ^= by
        moves.append((p, int(np.ravel_multi_index(place, dims))))
    return lax.ppermute(value, "pair", moves)


def is_paired(dims, times):
    return dims == (4, 2, 2) and times == 2 and PIECES == 2


def column_order(dims):
    depth, height, _ = dims
    order = [(0, 0)]
    for axis, size in ((0, depth), (1, height)):
        bit = size // 2
        while bit:
            order += [(z ^ bit, y) if axis == 0 else (z, y ^ bit) for z, y in order]
            bit //= 2
    return order


def plan_of(away, counts, dims, parts, joined):
    _, height, cores = dims
    source = jnp.zeros_like(away)
    index = jnp.zeros_like(away)
    spots = [(n, at) for n, part in enumerate(parts) for at in range(part)]
    for (z, y), (n, at) in zip(column_order(dims), spots):
        here = away // cores == z * height + y
        source = jnp.where(here, n * cores, source)
        index = jnp.where(here, at * joined, index)
    return jnp.concatenate([source + away % cores, index, lax.axis_index("tm")[None], counts]).astype(jnp.int32)


def after(values, others):
    return lax.optimization_barrier(tuple(values) + tuple(others))[: len(values)]


def join(held, more):
    (room,) = after([jnp.concatenate([held, held])], ())
    return lax.dynamic_update_slice(room, more, (held.shape[0], 0, 0))


def swap_times(value, step, times):
    return lax.ppermute(value, "tm", [((t + step) % times, t) for t in range(times)])


def gather_one(held, dims):
    depth, height, _ = dims
    for axis, size in ((0, depth), (1, height)):
        bit = size // 2
        while bit:
            held = jnp.concatenate([held, swap(held, dims, axis, bit)])
            bit //= 2
    return [held]


def gather_two(first, second, dims):
    first_far = swap(first, dims, 0, 2)
    (room,) = after([jnp.concatenate([first, first])], ())
    (second,) = after([second], [room])
    other = swap_times(second, 1, 2)
    pair = join(second, other)
    pair_far = swap(pair, dims, 0, 2)
    (first_two,) = after([lax.dynamic_update_slice(room, first_far, (1, 0, 0))], [pair])
    first_near = swap(first_two, dims, 0, 1)
    pair_two = jnp.concatenate([pair, pair_far])
    (first_near,) = after([first_near], [pair_two])
    first_four = jnp.concatenate([first_two, first_near])
    first_beside = swap(first_four, dims, 1, 1)
    pair_near = swap(pair_two, dims, 0, 1)
    pair_four = jnp.concatenate([pair_two, pair_near])
    first_core = swap(after([first_four], [pair_near])[0], dims, 2, 1)
    pair_beside = swap(pair_four, dims, 1, 1)
    return [first_four, first_beside], [pair_four, pair_beside], first_two, first_core


def both_cores(arrays, dims):
    if dims[2] == 1:
        return arrays
    return [value for array in arrays for value in (array, swap(array, dims, 2, 1))]


def shards(traces, owner, tiles, counts):
    seg_count, block, _ = traces.shape
    times = lax.axis_size("tm")
    segments = seg_count * times
    share = block // times
    slots = tiles.shape[0]
    bins = max(16, 128 // segments)
    groups = NF // bins
    rows = seg_count * 2 * bins
    wide = rows * times
    total = groups * rows
    part_rows = total // PIECES
    dims = chip_dims(lax.axis_size("pair"))
    smem = pl.BlockSpec(memory_space=pltpu.SMEM)
    anywhere = pl.BlockSpec(memory_space=pl.ANY)
    white = pl.pallas_call(
        functools.partial(whiten_kernel, bins),
        in_specs=[anywhere] * 2,
        out_shape=[jax.ShapeDtypeStruct((part_rows, block), jnp.bfloat16)] * PIECES,
        scratch_shapes=[
            pltpu.VMEM((CHUNKS, seg_count, block, NT // CHUNKS), jnp.float32),
            pltpu.VMEM((CHUNKS, 2 * NF, NT // CHUNKS), jnp.float32),
            pltpu.VMEM((NF + 16, seg_count * block), jnp.float32),
            pltpu.SemaphoreType.DMA((CHUNKS, 2)),
        ],
        compiler_params=pltpu.CompilerParams(vmem_limit_bytes=63 << 20),
        name="whiten",
    )(traces, jnp.asarray(forward_table()))

    paired = is_paired(dims, times)
    blocks = [own[None] for own in white]
    if paired:
        *gathered, near, swapped = gather_two(*blocks, dims)
        (tiles,) = after([tiles], [near])
    else:
        gathered = [gather_one(own, dims) for own in blocks]

    known = owner.shape[0]
    chosen = tiles.reshape(-1, 1) == jnp.arange(known, dtype=jnp.int32)
    stored = jnp.sum(jnp.where(chosen, owner, 0), axis=1)
    away = stored ^ lax.axis_index("pair")

    pack = part_rows + part_rows // block * share
    depth = 2 * NF // PIECES
    chunk = min(share, 16)
    inside = pl.BlockSpec(memory_space=pltpu.VMEM)
    operands = [
        pltpu.VMEM((share, groups // PIECES * wide), jnp.float32),
        pltpu.VMEM((groups // PIECES * wide, 2 * block), jnp.bfloat16),
    ]
    early = None
    for piece, arrays in enumerate(gathered):
        joined = times if paired and piece else 1
        plan = plan_of(away, counts, dims, [array.shape[0] // joined for array in arrays], joined)
        if joined > 1:
            arrays[-1:] = after(arrays[-1:], arrived[1:] + [table])
            arrived = both_cores(arrays, dims)
            continue
        sources = both_cores(arrays, dims)
        if paired:
            sources[1] = swapped
        arrived = list(pl.pallas_call(
            functools.partial(pick_kernel, len(sources)),
            in_specs=[smem] + [inside] * len(sources),
            out_shape=[jax.ShapeDtypeStruct((slots, pack, block), jnp.bfloat16)] * times,
            scratch_shapes=[
                pltpu.VMEM((slots, part_rows, block), jnp.bfloat16),
                pltpu.VMEM((slots, part_rows // block, block, block), jnp.bfloat16),
            ],
            compiler_params=pltpu.CompilerParams(vmem_limit_bytes=8 << 20),
            cost_estimate=pl.CostEstimate(flops=1, bytes_accessed=1, transcendentals=0),
            name="pick",
        )(plan, *sources))
        if not piece:
            table = inverse_table(segments, arrived[1:])
        for step in range(1, times):
            moves = [(t, (t + step) % times) for t in range(times)]
            arrived[step] = lax.ppermute(arrived[step], "tm", moves)
        if not piece:
            early = pl.pallas_call(
                functools.partial(cross_kernel, bins, rows, chunk),
                in_specs=[smem] + [inside] * times,
                out_shape=jax.ShapeDtypeStruct((slots, share // 2, depth, 2 * block), jnp.bfloat16),
                scratch_shapes=operands,
                compiler_params=pltpu.CompilerParams(vmem_limit_bytes=16 << 20),
                name="cross",
            )(plan, *arrived)

    return pl.pallas_call(
        functools.partial(stack_kernel, bins, rows, times, chunk, joined),
        in_specs=[smem] + [inside] * (2 + len(arrived)),
        out_specs=anywhere,
        out_shape=jax.ShapeDtypeStruct((slots, LAGS, share * block), jnp.float32),
        scratch_shapes=[
            pltpu.VMEM((slots, LAGS, share * block), jnp.float32),
            pltpu.VMEM((2, times, part_rows, block), jnp.bfloat16),
            pltpu.VMEM((block, part_rows), jnp.float32),
        ]
        + operands
        + [
            pltpu.VMEM((2, chunk // 2, depth, 2 * block), jnp.bfloat16),
            pltpu.SemaphoreType.DMA((slots, share // chunk)),
        ],
        compiler_params=pltpu.CompilerParams(vmem_limit_bytes=32 << 20),
        name="stack",
    )(plan, table, early, *arrived)


def solution(mesh):
    placed = (P("tm", "pair", None), P(), P("pair", None), P("pair"))
    return jax.shard_map(
        shards, mesh=mesh, in_specs=placed, out_specs=P("pair", None, "tm"), check_vma=False
    )
```

profile of v0, /device:TPU:1, one launch (start us, length us, event | category | flops | bytes accessed | tf_op | source)
XLA Modules:
  0.0 51.0 jit_solution(375546978879927360)
XLA Ops:
  0.0 3.2 %whiten.1 = (bf16[256,128]{1,0:T(8,128)(2,1)}, bf16[256,128]{1,0:T(8,128)(2,1)}) custom-call(f32[2,128,1024]{2,1,0:T(8,128)} %x_hbm.1, f32[256,1024]{1,0:T(8,128)} %constant.157.clone.table_hbm), custom_call_target="tpu_custom_call" | custom-call | tf_op jit(solution)/shard_map/whiten/pallas_call | solution.py:364
  3.2 3.2 %collective-permute-start = (bf16[1,256,128]{2,1,0:T(8,128)(2,1)}, bf16[1,256,128]{2,1,0:T(8,128)(2,1)S(1)}, u32[]{:S(2)}, u32[]{:S(2)}) collective-permute-start(bf16[1,256,128]{2,1,0:T(8,128)(2,1)} %bitcast.3), channel_id=1, source_target_pairs={{0,8},{1,9},{2,10},{3,11},{4,12},{5,13},{6,14},{7,15},{8,0},{9,1},... | collective-permute-start | bytes 196616 | tf_op jit(solution)/shard_map/ppermute | solution.py:270
  6.4 0.9 %pad_maximum_fusion.2 = bf16[2,256,128]{2,1,0:T(8,128)(2,1)S(1)} fusion(bf16[1,256,128]{2,1,0:T(8,128)(2,1)} %bitcast.4), kind=kLoop, calls=%fused_computation.10 | loop fusion | flops 65536 | bytes 196608 | tf_op jit(solution)/shard_map/concatenate | solution.py:325
  7.3 1.3 %collective-permute-start.1 = (bf16[1,256,128]{2,1,0:T(8,128)(2,1)}, bf16[1,256,128]{2,1,0:T(8,128)(2,1)S(1)}, u32[]{:S(2)}, u32[]{:S(2)}) collective-permute-start(bf16[1,256,128]{2,1,0:T(8,128)(2,1)} %bitcast.5), channel_id=1, source_target_pairs={{16,0},{0,16},{17,1},{1,17},{18,2},{2,18},{19,3},{3,19},{20,4},{4,... | collective-permute-start | bytes 196616 | tf_op jit(solution)/shard_map/ppermute | solution.py:310
  8.6 0.9 %pad_maximum_fusion.3 = bf16[2,256,128]{2,1,0:T(8,128)(2,1)S(1)} fusion(bf16[1,256,128]{2,1,0:T(8,128)(2,1)} %bitcast.6), kind=kLoop, calls=%fused_computation.11 | loop fusion | flops 65536 | bytes 196608 | tf_op jit(solution)/shard_map/concatenate | solution.py:305
  10.2 0.6 %collective-permute-done.1 = bf16[1,256,128]{2,1,0:T(8,128)(2,1)S(1)} collective-permute-done((bf16[1,256,128]{2,1,0:T(8,128)(2,1)}, bf16[1,256,128]{2,1,0:T(8,128)(2,1)S(1)}, u32[]{:S(2)}, u32[]{:S(2)}) %collective-permute-start.1) | collective-permute-done | bytes 65568 | tf_op jit(solution)/shard_map/ppermute | solution.py:310
  10.9 1.3 %collective-permute-start.2 = (bf16[2,256,128]{2,1,0:T(8,128)(2,1)S(1)}, bf16[2,256,128]{2,1,0:T(8,128)(2,1)S(1)}, u32[]{:S(2)}, u32[]{:S(2)}) collective-permute-start(bf16[2,256,128]{2,1,0:T(8,128)(2,1)S(1)} %constant_dynamic-update-slice_fusion.3), channel_id=1, source_target_pairs={{0,4},{1,5},{2,6},{3,7},{4,0},{5,1},{6,2},{7,3},{8,12},{9,13},{10,... | collective-permute-start | bytes 393224 | tf_op jit(solution)/shard_map/ppermute | solution.py:270
  12.2 0.8 %copy.8 = s32[3,2]{1,0:T(4,128)S(1)} copy(s32[3,2]{0,1:T(2,128)} %param.7) | data formatting | bytes 48 | tf_op jit(solution)/shard_map/optimization_barrier | solution.py:301
  13.1 0.8 %select_reduce_fusion = s32[6]{0:T(128)S(1)} fusion(s32[16]{0:T(128)} %param.6, s32[6]{0:T(128)S(1)} %eq.57), kind=kLoop, calls=%fused_computation.15 | loop fusion | flops 282 | bytes 112 | tf_op jit(solution)/shard_map/reduce_sum | solution.py:388
  13.9 3.7 %collective-permute-done.3 = bf16[2,256,128]{2,1,0:T(8,128)(2,1)S(1)} collective-permute-done((bf16[2,256,128]{2,1,0:T(8,128)(2,1)S(1)}, bf16[2,256,128]{2,1,0:T(8,128)(2,1)S(1)}, u32[]{:S(2)}, u32[]{:S(2)}) %collective-permute-start.3) | collective-permute-done | bytes 131104 | tf_op jit(solution)/shard_map/ppermute | solution.py:270
  17.7 1.7 %collective-permute-start.6 = (bf16[4,256,128]{2,1,0:T(8,128)(2,1)S(1)}, bf16[4,256,128]{2,1,0:T(8,128)(2,1)S(1)}, u32[]{:S(2)}, u32[]{:S(2)}) collective-permute-start(bf16[4,256,128]{2,1,0:T(8,128)(2,1)S(1)} %constant_dynamic-update-slice_fusion.refs_0_), channel_id=1, source_target_pairs={{0,2},{1,3},{2,0},{3,1},{4,6},{5,7},{6,4},{7,5},{8,10},{9,11},{10,... | collective-permute-start | bytes 786440 | tf_op jit(solution)/shard_map/ppermute | solution.py:270
  19.5 3.4 %collective-permute-done.4 = bf16[4,256,128]{2,1,0:T(8,128)(2,1)S(1)} collective-permute-done((bf16[4,256,128]{2,1,0:T(8,128)(2,1)S(1)}, bf16[4,256,128]{2,1,0:T(8,128)(2,1)S(1)}, u32[]{:S(2)}, u32[]{:S(2)}) %collective-permute-start.4) | collective-permute-done | bytes 262176 | tf_op jit(solution)/shard_map/ppermute | solution.py:270
  22.9 4.1 %collective-permute-start.5 = (bf16[4,256,128]{2,1,0:T(8,128)(2,1)S(1)}, bf16[4,256,128]{2,1,0:T(8,128)(2,1)S(1)}, u32[]{:S(2)}, u32[]{:S(2)}) collective-permute-start(bf16[4,256,128]{2,1,0:T(8,128)(2,1)S(1)} %constant_dynamic-update-slice_fusion.refs_0_), channel_id=1, source_target_pairs={{0,1},{1,0},{2,3},{3,2},{4,5},{5,4},{6,7},{7,6},{8,9},{9,8},{10,11... | collective-permute-start | bytes 786440 | tf_op jit(solution)/shard_map/ppermute | solution.py:270
  27.1 1.5 %collective-permute-start.10 = (bf16[8,256,128]{2,1,0:T(8,128)(2,1)S(1)}, bf16[8,256,128]{2,1,0:T(8,128)(2,1)S(1)}, u32[]{:S(2)}, u32[]{:S(2)}) collective-permute-start(bf16[8,256,128]{2,1,0:T(8,128)(2,1)S(1)} %pad_maximum_fusion.refs_0_), channel_id=1, source_target_pairs={{0,2},{1,3},{2,0},{3,1},{4,6},{5,7},{6,4},{7,5},{8,10},{9,11},{10,... | collective-permute-start | bytes 1572872 | tf_op jit(solution)/shard_map/ppermute | solution.py:270
  28.6 0.3 collective-permute-start.7
  28.9 1.2 %collective-permute-done.7.refs_3_ = bf16[4,256,128]{2,1,0:T(8,128)(2,1)S(1)} collective-permute-done((bf16[4,256,128]{2,1,0:T(8,128)(2,1)S(1)}, bf16[4,256,128]{2,1,0:T(8,128)(2,1)S(1)}, u32[]{:S(2)}, u32[]{:S(2)}) %collective-permute-start.7) | collective-permute-done | bytes 262176 | tf_op jit(solution)/shard_map/ppermute | solution.py:270
  30.1 1.0 %pick.1 = (bf16[3,384,128]{2,1,0:T(8,128)(2,1)S(1)}, bf16[3,384,128]{2,1,0:T(8,128)(2,1)S(1)}) custom-call(s32[14]{0:T(128)S(1)} %get-tuple-element.29.plan_ref, bf16[4,256,128]{2,1,0:T(8,128)(2,1)S(1)} %constant_dynamic-update-slice_fusion.refs_0_, bf16[4,256,128]{2,1,0:T(8,128)(2,1)S(1)} %collective-permute-done.5.refs_1_, ...), custom_call_target="tpu_custom_call" | custom-call | flops 1 | bytes 1 | tf_op jit(solution)/shard_map/pick/pallas_call | solution.py:410
  31.1 1.3 %collective-permute-start.8 = (bf16[3,384,128]{2,1,0:T(8,128)(2,1)S(1)}, bf16[3,384,128]{2,1,0:T(8,128)(2,1)S(1)}, u32[]{:S(2)}, u32[]{:S(2)}) collective-permute-start(bf16[3,384,128]{2,1,0:T(8,128)(2,1)S(1)} %get-tuple-element.23), channel_id=1, source_target_pairs={{0,16},{16,0},{1,17},{17,1},{2,18},{18,2},{3,19},{19,3},{4,20},{20... | collective-permute-start | bytes 884744 | tf_op jit(solution)/shard_map/ppermute | solution.py:426
  32.4 0.6 %collective-permute-start.9 = (bf16[8,256,128]{2,1,0:T(8,128)(2,1)S(1)}, bf16[8,256,128]{2,1,0:T(8,128)(2,1)S(1)}, u32[]{:S(2)}, u32[]{:S(2)}) collective-permute-start(bf16[8,256,128]{2,1,0:T(8,128)(2,1)S(1)} %pad_maximum_fusion.refs_0_), channel_id=1, source_target_pairs={{0,1},{1,0},{2,3},{3,2},{4,5},{5,4},{6,7},{7,6},{8,9},{9,8},{10,11... | collective-permute-start | bytes 1572872 | tf_op jit(solution)/shard_map/ppermute | solution.py:270
  32.9 0.6 %multiply_convert_fusion.table_ref = bf16[128,256]{1,0:T(8,128)(2,1)S(1)} fusion(s32[256]{0:T(256)S(1)} %fusion.5, s32[128]{0:T(128)S(1)} %iota_add_fusion, pred[256]{0:T(512)(128)(4,1)S(1)} %fusion.10), kind=kLoop, calls=%fused_computation.12 | loop fusion | flops 589824 | bytes 67328 | tf_op jit(solution)/shard_map/convert_element_type | solution.py:33
  33.5 7.1 %collective-permute-done.10.refs_2_ = bf16[8,256,128]{2,1,0:T(8,128)(2,1)S(1)} collective-permute-done((bf16[8,256,128]{2,1,0:T(8,128)(2,1)S(1)}, bf16[8,256,128]{2,1,0:T(8,128)(2,1)S(1)}, u32[]{:S(2)}, u32[]{:S(2)}) %collective-permute-start.10) | collective-permute-done | bytes 524320 | tf_op jit(solution)/shard_map/ppermute | solution.py:270
  40.7 0.8 %collective-permute-start.11 = (bf16[8,256,128]{2,1,0:T(8,128)(2,1)S(1)}, bf16[8,256,128]{2,1,0:T(8,128)(2,1)S(1)}, u32[]{:S(2)}, u32[]{:S(2)}) collective-permute-start(bf16[8,256,128]{2,1,0:T(8,128)(2,1)S(1)} %collective-permute-done.10.refs_2_), channel_id=1, source_target_pairs={{0,1},{1,0},{2,3},{3,2},{4,5},{5,4},{6,7},{7,6},{8,9},{9,8},{10,11... | collective-permute-start | bytes 1572872 | tf_op jit(solution)/shard_map/ppermute | solution.py:270
  41.5 2.8 %cross.1.early_ref = bf16[3,32,128,256]{3,2,1,0:T(8,128)(2,1)S(1)} custom-call(s32[14]{0:T(128)S(1)} %get-tuple-element.29.plan_ref, bf16[3,384,128]{2,1,0:T(8,128)(2,1)S(1)} %get-tuple-element.25.refs_0_, bf16[3,384,128]{2,1,0:T(8,128)(2,1)S(1)} %collective-permute-done.8.refs_1_), custom_call_target="tpu_custom_call" | custom-call | tf_op jit(solution)/shard_map/cross/pallas_call | solution.py:428
  44.3 6.8 %stack.1 = f32[3,128,8192]{2,1,0:T(8,128)} custom-call(s32[14]{0:T(128)S(1)} %get-tuple-element.30.plan_ref, bf16[128,256]{1,0:T(8,128)(2,1)S(1)} %multiply_convert_fusion.table_ref, bf16[3,32,128,256]{3,2,1,0:T(8,128)(2,1)S(1)} %cross.1.early_ref, bf16[8,256,128]{2,1,0:T(8,128)(2,1)S(1)} %pad_maximum_fusion.refs_0_, ...), custom_call_target="tpu_custom_call" | custom-call | tf_op jit(solution)/shard_map/stack/pallas_call | solution.py:437
  (22 shorter events, 0.5 us)
Async XLA Ops:
  3.2 7.7 %collective-permute-start = (bf16[1,256,128]{2,1,0:T(8,128)(2,1)}, bf16[1,256,128]{2,1,0:T(8,128)(2,1)S(1)}, u32[]{:S(2)}, u32[]{:S(2)}) collective-permute-start(bf16[1,256,128]{2,1,0:T(8,128)(2,1)} %bitcast.3), channel_id=1, source_target_pairs={{0,8},{1,9},{2,10},{3,11},{4,12},{5,13},{6,14},{7,15},{8,0},{9,1},... | collective-permute-start | bytes 196616 | tf_op jit(solution)/shard_map/ppermute | solution.py:270
  7.3 3.5 %collective-permute-start.1 = (bf16[1,256,128]{2,1,0:T(8,128)(2,1)}, bf16[1,256,128]{2,1,0:T(8,128)(2,1)S(1)}, u32[]{:S(2)}, u32[]{:S(2)}) collective-permute-start(bf16[1,256,128]{2,1,0:T(8,128)(2,1)} %bitcast.5), channel_id=1, source_target_pairs={{16,0},{0,16},{17,1},{1,17},{18,2},{2,18},{19,3},{3,19},{20,4},{4,... | collective-permute-start | bytes 196616 | tf_op jit(solution)/shard_map/ppermute | solution.py:310
  10.8 6.8 %collective-permute-start.3 = (bf16[2,256,128]{2,1,0:T(8,128)(2,1)S(1)}, bf16[2,256,128]{2,1,0:T(8,128)(2,1)S(1)}, u32[]{:S(2)}, u32[]{:S(2)}) collective-permute-start(bf16[2,256,128]{2,1,0:T(8,128)(2,1)S(1)} %constant_dynamic-update-slice_fusion.2), channel_id=1, source_target_pairs={{0,8},{1,9},{2,10},{3,11},{4,12},{5,13},{6,14},{7,15},{8,0},{9,1},... | collective-permute-start | bytes 393224 | tf_op jit(solution)/shard_map/ppermute | solution.py:270
  10.9 6.8 %collective-permute-start.2 = (bf16[2,256,128]{2,1,0:T(8,128)(2,1)S(1)}, bf16[2,256,128]{2,1,0:T(8,128)(2,1)S(1)}, u32[]{:S(2)}, u32[]{:S(2)}) collective-permute-start(bf16[2,256,128]{2,1,0:T(8,128)(2,1)S(1)} %constant_dynamic-update-slice_fusion.3), channel_id=1, source_target_pairs={{0,4},{1,5},{2,6},{3,7},{4,0},{5,1},{6,2},{7,3},{8,12},{9,13},{10,... | collective-permute-start | bytes 393224 | tf_op jit(solution)/shard_map/ppermute | solution.py:270
  17.6 5.3 %collective-permute-start.4 = (bf16[4,256,128]{2,1,0:T(8,128)(2,1)S(1)}, bf16[4,256,128]{2,1,0:T(8,128)(2,1)S(1)}, u32[]{:S(2)}, u32[]{:S(2)}) collective-permute-start(bf16[4,256,128]{2,1,0:T(8,128)(2,1)S(1)} %pad_maximum_fusion.1), channel_id=1, source_target_pairs={{0,4},{1,5},{2,6},{3,7},{4,0},{5,1},{6,2},{7,3},{8,12},{9,13},{10,... | collective-permute-start | bytes 786440 | tf_op jit(solution)/shard_map/ppermute | solution.py:270
  17.7 10.8 %collective-permute-start.6 = (bf16[4,256,128]{2,1,0:T(8,128)(2,1)S(1)}, bf16[4,256,128]{2,1,0:T(8,128)(2,1)S(1)}, u32[]{:S(2)}, u32[]{:S(2)}) collective-permute-start(bf16[4,256,128]{2,1,0:T(8,128)(2,1)S(1)} %constant_dynamic-update-slice_fusion.refs_0_), channel_id=1, source_target_pairs={{0,2},{1,3},{2,0},{3,1},{4,6},{5,7},{6,4},{7,5},{8,10},{9,11},{10,... | collective-permute-start | bytes 786440 | tf_op jit(solution)/shard_map/ppermute | solution.py:270
  22.9 7.2 %collective-permute-start.5 = (bf16[4,256,128]{2,1,0:T(8,128)(2,1)S(1)}, bf16[4,256,128]{2,1,0:T(8,128)(2,1)S(1)}, u32[]{:S(2)}, u32[]{:S(2)}) collective-permute-start(bf16[4,256,128]{2,1,0:T(8,128)(2,1)S(1)} %constant_dynamic-update-slice_fusion.refs_0_), channel_id=1, source_target_pairs={{0,1},{1,0},{2,3},{3,2},{4,5},{5,4},{6,7},{7,6},{8,9},{9,8},{10,11... | collective-permute-start | bytes 786440 | tf_op jit(solution)/shard_map/ppermute | solution.py:270
  27.1 13.6 %collective-permute-start.10 = (bf16[8,256,128]{2,1,0:T(8,128)(2,1)S(1)}, bf16[8,256,128]{2,1,0:T(8,128)(2,1)S(1)}, u32[]{:S(2)}, u32[]{:S(2)}) collective-permute-start(bf16[8,256,128]{2,1,0:T(8,128)(2,1)S(1)} %pad_maximum_fusion.refs_0_), channel_id=1, source_target_pairs={{0,2},{1,3},{2,0},{3,1},{4,6},{5,7},{6,4},{7,5},{8,10},{9,11},{10,... | collective-permute-start | bytes 1572872 | tf_op jit(solution)/shard_map/ppermute | solution.py:270
  28.6 1.5 %collective-permute-start.7 = (bf16[4,256,128]{2,1,0:T(8,128)(2,1)S(1)}, bf16[4,256,128]{2,1,0:T(8,128)(2,1)S(1)}, u32[]{:S(2)}, u32[]{:S(2)}) collective-permute-start(bf16[4,256,128]{2,1,0:T(8,128)(2,1)S(1)} %collective-permute-done.6.refs_2_), channel_id=1, source_target_pairs={{0,1},{1,0},{2,3},{3,2},{4,5},{5,4},{6,7},{7,6},{8,9},{9,8},{10,11... | collective-permute-start | bytes 786440 | tf_op jit(solution)/shard_map/ppermute | solution.py:270
  31.1 9.6 %collective-permute-start.8 = (bf16[3,384,128]{2,1,0:T(8,128)(2,1)S(1)}, bf16[3,384,128]{2,1,0:T(8,128)(2,1)S(1)}, u32[]{:S(2)}, u32[]{:S(2)}) collective-permute-start(bf16[3,384,128]{2,1,0:T(8,128)(2,1)S(1)} %get-tuple-element.23), channel_id=1, source_target_pairs={{0,16},{16,0},{1,17},{17,1},{2,18},{18,2},{3,19},{19,3},{4,20},{20... | collective-permute-start | bytes 884744 | tf_op jit(solution)/shard_map/ppermute | solution.py:426
  32.4 11.9 %collective-permute-start.9 = (bf16[8,256,128]{2,1,0:T(8,128)(2,1)S(1)}, bf16[8,256,128]{2,1,0:T(8,128)(2,1)S(1)}, u32[]{:S(2)}, u32[]{:S(2)}) collective-permute-start(bf16[8,256,128]{2,1,0:T(8,128)(2,1)S(1)} %pad_maximum_fusion.refs_0_), channel_id=1, source_target_pairs={{0,1},{1,0},{2,3},{3,2},{4,5},{5,4},{6,7},{7,6},{8,9},{9,8},{10,11... | collective-permute-start | bytes 1572872 | tf_op jit(solution)/shard_map/ppermute | solution.py:270
  40.7 3.6 %collective-permute-start.11 = (bf16[8,256,128]{2,1,0:T(8,128)(2,1)S(1)}, bf16[8,256,128]{2,1,0:T(8,128)(2,1)S(1)}, u32[]{:S(2)}, u32[]{:S(2)}) collective-permute-start(bf16[8,256,128]{2,1,0:T(8,128)(2,1)S(1)} %collective-permute-done.10.refs_2_), channel_id=1, source_target_pairs={{0,1},{1,0},{2,3},{3,2},{4,5},{5,4},{6,7},{7,6},{8,9},{9,8},{10,11... | collective-permute-start | bytes 1572872 | tf_op jit(solution)/shard_map/ppermute | solution.py:270
where the time goes:
time: 50.3 us; the launch traced here: 51 us
  starting transfers between devices  16.2 us (32%)
  waiting for transfers between devices  16 us (32%)
  Pallas kernels  13.6 us (27%)
  other arithmetic  3.49 us (7%)
  local copies, waits for them, and re-layouts  0.91 us (2%)
  between operations  0.77 us (2%)
    ppermute x10, waiting for transfers between devices, swap(): return lax.ppermute(value, 'pair', moves)  15.4 us
    ppermute x10, starting transfers between devices, swap(): return lax.ppermute(value, 'pair', moves)  13.6 us
    pallas_call x1, Pallas kernels, shards(): pl.pallas_call(functools.partial(stack_kernel, bins, rows, times, chunk,...  6.75 us
    pallas_call x1, Pallas kernels, shards(): pl.pallas_call(functools.partial(whiten_kernel, bins), in_specs=[anywhere...  3.17 us
    pallas_call x1, Pallas kernels, shards(): pl.pallas_call(functools.partial(cross_kernel, bins, rows, chunk), in_spe...  2.77 us
    ppermute x1, starting transfers between devices, shards(): arrived[step] = lax.ppermute(arrived[step], 'tm', moves)  1.28 us
    ppermute x1, starting transfers between devices, swap_times(): lax.ppermute(value, 'tm', [((t + step) % times, t) for t in range(times)])  1.28 us
  transfers between devices with their start and end apart: 12, of which 5 were waited for; matrix products, arithmetic and copies ran while one was open for 9% of the time, Pallas kernels for 7%

commit v1 on v0

--- a/solution.py
+++ b/solution.py
@@ -335,9 +335,8 @@
     first_beside = swap(first_four, dims, 1, 1)
     pair_near = swap(pair_two, dims, 0, 1)
     pair_four = jnp.concatenate([pair_two, pair_near])
-    first_core = swap(after([first_four], [pair_near])[0], dims, 2, 1)
     pair_beside = swap(pair_four, dims, 1, 1)
-    return [first_four, first_beside], [pair_four, pair_beside], first_two, first_core
+    return [first_four, first_beside], [pair_four, pair_beside], first_two
 
 
 def both_cores(arrays, dims):
@@ -378,7 +377,7 @@
     paired = is_paired(dims, times)
     blocks = [own[None] for own in white]
     if paired:
-        *gathered, near, swapped = gather_two(*blocks, dims)
+        *gathered, near = gather_two(*blocks, dims)
         (tiles,) = after([tiles], [near])
     else:
         gathered = [gather_one(own, dims) for own in blocks]
@@ -405,8 +404,6 @@
             arrived = both_cores(arrays, dims)
             continue
         sources = both_cores(arrays, dims)
-        if paired:
-            sources[1] = swapped
         arrived = list(pl.pallas_call(
             functools.partial(pick_kernel, len(sources)),
             in_specs=[smem] + [inside] * len(sources),

time: 50.3 us -> 50.6 us (level)
  the two profiles are of different devices: /device:TPU:1 before, /device:TPU:0 now
where the time goes in v1:
time: 50.6 us; the launch traced here: 50 us
  waiting for transfers between devices  18.2 us (36%)
  Pallas kernels  13.6 us (27%)
  starting transfers between devices  13 us (26%)
  other arithmetic  3.49 us (7%)
  local copies, waits for them, and re-layouts  0.91 us (2%)
  between operations  0.76 us (2%)
    ppermute x10, waiting for transfers between devices, swap(): return lax.ppermute(value, 'pair', moves)  14.8 us
    ppermute x10, starting transfers between devices, swap(): return lax.ppermute(value, 'pair', moves)  9.84 us
    pallas_call x1, Pallas kernels, shards(): pl.pallas_call(functools.partial(stack_kernel, bins, rows, times, chunk,...  6.75 us
    pallas_call x1, Pallas kernels, shards(): pl.pallas_call(functools.partial(whiten_kernel, bins), in_specs=[anywhere...  3.17 us
    pallas_call x1, Pallas kernels, shards(): pl.pallas_call(functools.partial(cross_kernel, bins, rows, chunk), in_spe...  2.77 us
    ppermute x1, waiting for transfers between devices, shards(): arrived[step] = lax.ppermute(arrived[step], 'tm', moves)  1.95 us
    ppermute x1, starting transfers between devices, shards(): arrived[step] = lax.ppermute(arrived[step], 'tm', moves)  1.56 us
    ppermute x1, starting transfers between devices, swap_times(): lax.ppermute(value, 'tm', [((t + step) % times, t) for t in range(times)])  1.56 us
  transfers between devices with their start and end apart: 12, of which 6 were waited for; matrix products, arithmetic and copies ran while one was open for 9% of the time, Pallas kernels for 7%

profile of v1, /device:TPU:0, one launch (start us, length us, event | category | flops | bytes accessed | tf_op | source)
XLA Modules:
  0.0 50.0 jit_solution(17823842335690454119)
XLA Ops:
  0.0 3.2 %whiten.1 = (bf16[256,128]{1,0:T(8,128)(2,1)}, bf16[256,128]{1,0:T(8,128)(2,1)}) custom-call(f32[2,128,1024]{2,1,0:T(8,128)} %x_hbm.1, f32[256,1024]{1,0:T(8,128)} %constant.157.clone.table_hbm), custom_call_target="tpu_custom_call" | custom-call | tf_op jit(solution)/shard_map/whiten/pallas_call | solution.py:363
  3.2 4.1 %collective-permute-start = (bf16[1,256,128]{2,1,0:T(8,128)(2,1)}, bf16[1,256,128]{2,1,0:T(8,128)(2,1)S(1)}, u32[]{:S(2)}, u32[]{:S(2)}) collective-permute-start(bf16[1,256,128]{2,1,0:T(8,128)(2,1)} %bitcast.3), channel_id=1, source_target_pairs={{0,8},{1,9},{2,10},{3,11},{4,12},{5,13},{6,14},{7,15},{8,0},{9,1},... | collective-permute-start | bytes 196616 | tf_op jit(solution)/shard_map/ppermute | solution.py:270
  7.3 0.9 %pad_maximum_fusion.2 = bf16[2,256,128]{2,1,0:T(8,128)(2,1)S(1)} fusion(bf16[1,256,128]{2,1,0:T(8,128)(2,1)} %bitcast.4), kind=kLoop, calls=%fused_computation.10 | loop fusion | flops 65536 | bytes 196608 | tf_op jit(solution)/shard_map/concatenate | solution.py:325
  8.2 1.6 %collective-permute-start.1 = (bf16[1,256,128]{2,1,0:T(8,128)(2,1)}, bf16[1,256,128]{2,1,0:T(8,128)(2,1)S(1)}, u32[]{:S(2)}, u32[]{:S(2)}) collective-permute-start(bf16[1,256,128]{2,1,0:T(8,128)(2,1)} %bitcast.5), channel_id=1, source_target_pairs={{16,0},{0,16},{17,1},{1,17},{18,2},{2,18},{19,3},{3,19},{20,4},{4,... | collective-permute-start | bytes 196616 | tf_op jit(solution)/shard_map/ppermute | solution.py:310
  9.8 0.9 %pad_maximum_fusion.3 = bf16[2,256,128]{2,1,0:T(8,128)(2,1)S(1)} fusion(bf16[1,256,128]{2,1,0:T(8,128)(2,1)} %bitcast.6), kind=kLoop, calls=%fused_computation.11 | loop fusion | flops 65536 | bytes 196608 | tf_op jit(solution)/shard_map/concatenate | solution.py:305
  11.3 1.4 %collective-permute-done.1 = bf16[1,256,128]{2,1,0:T(8,128)(2,1)S(1)} collective-permute-done((bf16[1,256,128]{2,1,0:T(8,128)(2,1)}, bf16[1,256,128]{2,1,0:T(8,128)(2,1)S(1)}, u32[]{:S(2)}, u32[]{:S(2)}) %collective-permute-start.1) | collective-permute-done | bytes 65568 | tf_op jit(solution)/shard_map/ppermute | solution.py:310
  12.9 2.0 %collective-permute-start.2 = (bf16[2,256,128]{2,1,0:T(8,128)(2,1)S(1)}, bf16[2,256,128]{2,1,0:T(8,128)(2,1)S(1)}, u32[]{:S(2)}, u32[]{:S(2)}) collective-permute-start(bf16[2,256,128]{2,1,0:T(8,128)(2,1)S(1)} %constant_dynamic-update-slice_fusion.3), channel_id=1, source_target_pairs={{0,4},{1,5},{2,6},{3,7},{4,0},{5,1},{6,2},{7,3},{8,12},{9,13},{10,... | collective-permute-start | bytes 393224 | tf_op jit(solution)/shard_map/ppermute | solution.py:270
  14.8 0.8 %copy.8 = s32[3,2]{1,0:T(4,128)S(1)} copy(s32[3,2]{0,1:T(2,128)} %param.7) | data formatting | bytes 48 | tf_op jit(solution)/shard_map/optimization_barrier | solution.py:301
  15.6 0.1 eq.57
  15.7 0.8 %select_reduce_fusion = s32[6]{0:T(128)S(1)} fusion(s32[16]{0:T(128)} %param.6, s32[6]{0:T(128)S(1)} %eq.57), kind=kLoop, calls=%fused_computation.15 | loop fusion | flops 282 | bytes 112 | tf_op jit(solution)/shard_map/reduce_sum | solution.py:387
  16.5 4.0 %collective-permute-done.3 = bf16[2,256,128]{2,1,0:T(8,128)(2,1)S(1)} collective-permute-done((bf16[2,256,128]{2,1,0:T(8,128)(2,1)S(1)}, bf16[2,256,128]{2,1,0:T(8,128)(2,1)S(1)}, u32[]{:S(2)}, u32[]{:S(2)}) %collective-permute-start.3) | collective-permute-done | bytes 131104 | tf_op jit(solution)/shard_map/ppermute | solution.py:270
  20.5 0.2 collective-permute-start.8
  20.8 1.6 %collective-permute-start.5 = (bf16[4,256,128]{2,1,0:T(8,128)(2,1)S(1)}, bf16[4,256,128]{2,1,0:T(8,128)(2,1)S(1)}, u32[]{:S(2)}, u32[]{:S(2)}) collective-permute-start(bf16[4,256,128]{2,1,0:T(8,128)(2,1)S(1)} %constant_dynamic-update-slice_fusion.refs_0_), channel_id=1, source_target_pairs={{0,2},{1,3},{2,0},{3,1},{4,6},{5,7},{6,4},{7,5},{8,10},{9,11},{10,... | collective-permute-start | bytes 786440 | tf_op jit(solution)/shard_map/ppermute | solution.py:270
  22.5 4.5 %collective-permute-done.8 = bf16[4,256,128]{2,1,0:T(8,128)(2,1)S(1)} collective-permute-done((bf16[4,256,128]{2,1,0:T(8,128)(2,1)S(1)}, bf16[4,256,128]{2,1,0:T(8,128)(2,1)S(1)}, u32[]{:S(2)}, u32[]{:S(2)}) %collective-permute-start.8) | collective-permute-done | bytes 262176 | tf_op jit(solution)/shard_map/ppermute | solution.py:270
  27.0 1.8 %collective-permute-start.10 = (bf16[8,256,128]{2,1,0:T(8,128)(2,1)S(1)}, bf16[8,256,128]{2,1,0:T(8,128)(2,1)S(1)}, u32[]{:S(2)}, u32[]{:S(2)}) collective-permute-start(bf16[8,256,128]{2,1,0:T(8,128)(2,1)S(1)} %pad_maximum_fusion.refs_0_), channel_id=1, source_target_pairs={{0,2},{1,3},{2,0},{3,1},{4,6},{5,7},{6,4},{7,5},{8,10},{9,11},{10,... | collective-permute-start | bytes 1572872 | tf_op jit(solution)/shard_map/ppermute | solution.py:270
  28.8 0.1 add_add_fusion.1
  28.9 1.4 %collective-permute-done.6.refs_3_ = bf16[4,256,128]{2,1,0:T(8,128)(2,1)S(1)} collective-permute-done((bf16[4,256,128]{2,1,0:T(8,128)(2,1)S(1)}, bf16[4,256,128]{2,1,0:T(8,128)(2,1)S(1)}, u32[]{:S(2)}, u32[]{:S(2)}) %collective-permute-start.6) | collective-permute-done | bytes 262176 | tf_op jit(solution)/shard_map/ppermute | solution.py:270
  30.3 1.0 %pick.1 = (bf16[3,384,128]{2,1,0:T(8,128)(2,1)S(1)}, bf16[3,384,128]{2,1,0:T(8,128)(2,1)S(1)}) custom-call(s32[14]{0:T(128)S(1)} %get-tuple-element.27.plan_ref, bf16[4,256,128]{2,1,0:T(8,128)(2,1)S(1)} %constant_dynamic-update-slice_fusion.refs_0_, bf16[4,256,128]{2,1,0:T(8,128)(2,1)S(1)} %collective-permute-done.4.refs_1_, ...), custom_call_target="tpu_custom_call" | custom-call | flops 1 | bytes 1 | tf_op jit(solution)/shard_map/pick/pallas_call | solution.py:407
  31.3 1.6 %collective-permute-start.7 = (bf16[3,384,128]{2,1,0:T(8,128)(2,1)S(1)}, bf16[3,384,128]{2,1,0:T(8,128)(2,1)S(1)}, u32[]{:S(2)}, u32[]{:S(2)}) collective-permute-start(bf16[3,384,128]{2,1,0:T(8,128)(2,1)S(1)} %get-tuple-element.21), channel_id=1, source_target_pairs={{0,16},{16,0},{1,17},{17,1},{2,18},{18,2},{3,19},{19,3},{4,20},{20... | collective-permute-start | bytes 884744 | tf_op jit(solution)/shard_map/ppermute | solution.py:423
  32.9 0.6 %multiply_convert_fusion.table_ref = bf16[128,256]{1,0:T(8,128)(2,1)S(1)} fusion(s32[256]{0:T(256)S(1)} %fusion.5, s32[128]{0:T(128)S(1)} %iota_add_fusion, pred[256]{0:T(512)(128)(4,1)S(1)} %fusion.10), kind=kLoop, calls=%fused_computation.12 | loop fusion | flops 589824 | bytes 67328 | tf_op jit(solution)/shard_map/convert_element_type | solution.py:33
  33.5 5.0 %collective-permute-done.10.refs_2_ = bf16[8,256,128]{2,1,0:T(8,128)(2,1)S(1)} collective-permute-done((bf16[8,256,128]{2,1,0:T(8,128)(2,1)S(1)}, bf16[8,256,128]{2,1,0:T(8,128)(2,1)S(1)}, u32[]{:S(2)}, u32[]{:S(2)}) %collective-permute-start.10) | collective-permute-done | bytes 524320 | tf_op jit(solution)/shard_map/ppermute | solution.py:270
  38.4 1.9 %collective-permute-done.7.refs_1_ = bf16[3,384,128]{2,1,0:T(8,128)(2,1)S(1)} collective-permute-done((bf16[3,384,128]{2,1,0:T(8,128)(2,1)S(1)}, bf16[3,384,128]{2,1,0:T(8,128)(2,1)S(1)}, u32[]{:S(2)}, u32[]{:S(2)}) %collective-permute-start.7) | collective-permute-done | bytes 294944 | tf_op jit(solution)/shard_map/ppermute | solution.py:423
  40.4 2.8 %cross.1.early_ref = bf16[3,32,128,256]{3,2,1,0:T(8,128)(2,1)S(1)} custom-call(s32[14]{0:T(128)S(1)} %get-tuple-element.27.plan_ref, bf16[3,384,128]{2,1,0:T(8,128)(2,1)S(1)} %get-tuple-element.23.refs_0_, bf16[3,384,128]{2,1,0:T(8,128)(2,1)S(1)} %collective-permute-done.7.refs_1_), custom_call_target="tpu_custom_call" | custom-call | tf_op jit(solution)/shard_map/cross/pallas_call | solution.py:425
  43.2 6.8 %stack.1 = f32[3,128,8192]{2,1,0:T(8,128)} custom-call(s32[14]{0:T(128)S(1)} %get-tuple-element.28.plan_ref, bf16[128,256]{1,0:T(8,128)(2,1)S(1)} %multiply_convert_fusion.table_ref, bf16[3,32,128,256]{3,2,1,0:T(8,128)(2,1)S(1)} %cross.1.early_ref, bf16[8,256,128]{2,1,0:T(8,128)(2,1)S(1)} %pad_maximum_fusion.refs_0_, ...), custom_call_target="tpu_custom_call" | custom-call | tf_op jit(solution)/shard_map/stack/pallas_call | solution.py:434
  (22 shorter events, 0.3 us)
Async XLA Ops:
  3.2 9.7 %collective-permute-start = (bf16[1,256,128]{2,1,0:T(8,128)(2,1)}, bf16[1,256,128]{2,1,0:T(8,128)(2,1)S(1)}, u32[]{:S(2)}, u32[]{:S(2)}) collective-permute-start(bf16[1,256,128]{2,1,0:T(8,128)(2,1)} %bitcast.3), channel_id=1, source_target_pairs={{0,8},{1,9},{2,10},{3,11},{4,12},{5,13},{6,14},{7,15},{8,0},{9,1},... | collective-permute-start | bytes 196616 | tf_op jit(solution)/shard_map/ppermute | solution.py:270
  8.2 4.5 %collective-permute-start.1 = (bf16[1,256,128]{2,1,0:T(8,128)(2,1)}, bf16[1,256,128]{2,1,0:T(8,128)(2,1)S(1)}, u32[]{:S(2)}, u32[]{:S(2)}) collective-permute-start(bf16[1,256,128]{2,1,0:T(8,128)(2,1)} %bitcast.5), channel_id=1, source_target_pairs={{16,0},{0,16},{17,1},{1,17},{18,2},{2,18},{19,3},{3,19},{20,4},{4,... | collective-permute-start | bytes 196616 | tf_op jit(solution)/shard_map/ppermute | solution.py:310
  12.8 7.7 %collective-permute-start.3 = (bf16[2,256,128]{2,1,0:T(8,128)(2,1)S(1)}, bf16[2,256,128]{2,1,0:T(8,128)(2,1)S(1)}, u32[]{:S(2)}, u32[]{:S(2)}) collective-permute-start(bf16[2,256,128]{2,1,0:T(8,128)(2,1)S(1)} %constant_dynamic-update-slice_fusion.2), channel_id=1, source_target_pairs={{0,8},{1,9},{2,10},{3,11},{4,12},{5,13},{6,14},{7,15},{8,0},{9,1},... | collective-permute-start | bytes 393224 | tf_op jit(solution)/shard_map/ppermute | solution.py:270
  12.9 7.9 %collective-permute-start.2 = (bf16[2,256,128]{2,1,0:T(8,128)(2,1)S(1)}, bf16[2,256,128]{2,1,0:T(8,128)(2,1)S(1)}, u32[]{:S(2)}, u32[]{:S(2)}) collective-permute-start(bf16[2,256,128]{2,1,0:T(8,128)(2,1)S(1)} %constant_dynamic-update-slice_fusion.3), channel_id=1, source_target_pairs={{0,4},{1,5},{2,6},{3,7},{4,0},{5,1},{6,2},{7,3},{8,12},{9,13},{10,... | collective-permute-start | bytes 393224 | tf_op jit(solution)/shard_map/ppermute | solution.py:270
  20.5 6.4 %collective-permute-start.8 = (bf16[4,256,128]{2,1,0:T(8,128)(2,1)S(1)}, bf16[4,256,128]{2,1,0:T(8,128)(2,1)S(1)}, u32[]{:S(2)}, u32[]{:S(2)}) collective-permute-start(bf16[4,256,128]{2,1,0:T(8,128)(2,1)S(1)} %pad_maximum_fusion.1), channel_id=1, source_target_pairs={{0,4},{1,5},{2,6},{3,7},{4,0},{5,1},{6,2},{7,3},{8,12},{9,13},{10,... | collective-permute-start | bytes 786440 | tf_op jit(solution)/shard_map/ppermute | solution.py:270
  20.8 8.0 %collective-permute-start.5 = (bf16[4,256,128]{2,1,0:T(8,128)(2,1)S(1)}, bf16[4,256,128]{2,1,0:T(8,128)(2,1)S(1)}, u32[]{:S(2)}, u32[]{:S(2)}) collective-permute-start(bf16[4,256,128]{2,1,0:T(8,128)(2,1)S(1)} %constant_dynamic-update-slice_fusion.refs_0_), channel_id=1, source_target_pairs={{0,2},{1,3},{2,0},{3,1},{4,6},{5,7},{6,4},{7,5},{8,10},{9,11},{10,... | collective-permute-start | bytes 786440 | tf_op jit(solution)/shard_map/ppermute | solution.py:270
  22.4 6.5 %collective-permute-start.4 = (bf16[4,256,128]{2,1,0:T(8,128)(2,1)S(1)}, bf16[4,256,128]{2,1,0:T(8,128)(2,1)S(1)}, u32[]{:S(2)}, u32[]{:S(2)}) collective-permute-start(bf16[4,256,128]{2,1,0:T(8,128)(2,1)S(1)} %constant_dynamic-update-slice_fusion.refs_0_), channel_id=1, source_target_pairs={{0,1},{1,0},{2,3},{3,2},{4,5},{5,4},{6,7},{7,6},{8,9},{9,8},{10,11... | collective-permute-start | bytes 786440 | tf_op jit(solution)/shard_map/ppermute | solution.py:270
  27.0 11.4 %collective-permute-start.10 = (bf16[8,256,128]{2,1,0:T(8,128)(2,1)S(1)}, bf16[8,256,128]{2,1,0:T(8,128)(2,1)S(1)}, u32[]{:S(2)}, u32[]{:S(2)}) collective-permute-start(bf16[8,256,128]{2,1,0:T(8,128)(2,1)S(1)} %pad_maximum_fusion.refs_0_), channel_id=1, source_target_pairs={{0,2},{1,3},{2,0},{3,1},{4,6},{5,7},{6,4},{7,5},{8,10},{9,11},{10,... | collective-permute-start | bytes 1572872 | tf_op jit(solution)/shard_map/ppermute | solution.py:270
  28.8 1.5 %collective-permute-start.6 = (bf16[4,256,128]{2,1,0:T(8,128)(2,1)S(1)}, bf16[4,256,128]{2,1,0:T(8,128)(2,1)S(1)}, u32[]{:S(2)}, u32[]{:S(2)}) collective-permute-start(bf16[4,256,128]{2,1,0:T(8,128)(2,1)S(1)} %collective-permute-done.5.refs_2_), channel_id=1, source_target_pairs={{0,1},{1,0},{2,3},{3,2},{4,5},{5,4},{6,7},{7,6},{8,9},{9,8},{10,11... | collective-permute-start | bytes 786440 | tf_op jit(solution)/shard_map/ppermute | solution.py:270
  31.3 9.1 %collective-permute-start.7 = (bf16[3,384,128]{2,1,0:T(8,128)(2,1)S(1)}, bf16[3,384,128]{2,1,0:T(8,128)(2,1)S(1)}, u32[]{:S(2)}, u32[]{:S(2)}) collective-permute-start(bf16[3,384,128]{2,1,0:T(8,128)(2,1)S(1)} %get-tuple-element.21), channel_id=1, source_target_pairs={{0,16},{16,0},{1,17},{17,1},{2,18},{18,2},{3,19},{19,3},{4,20},{20... | collective-permute-start | bytes 884744 | tf_op jit(solution)/shard_map/ppermute | solution.py:423
  32.9 10.3 %collective-permute-start.9 = (bf16[8,256,128]{2,1,0:T(8,128)(2,1)S(1)}, bf16[8,256,128]{2,1,0:T(8,128)(2,1)S(1)}, u32[]{:S(2)}, u32[]{:S(2)}) collective-permute-start(bf16[8,256,128]{2,1,0:T(8,128)(2,1)S(1)} %pad_maximum_fusion.refs_0_), channel_id=1, source_target_pairs={{0,1},{1,0},{2,3},{3,2},{4,5},{5,4},{6,7},{7,6},{8,9},{9,8},{10,11... | collective-permute-start | bytes 1572872 | tf_op jit(solution)/shard_map/ppermute | solution.py:270
  40.4 2.8 %collective-permute-start.11 = (bf16[8,256,128]{2,1,0:T(8,128)(2,1)S(1)}, bf16[8,256,128]{2,1,0:T(8,128)(2,1)S(1)}, u32[]{:S(2)}, u32[]{:S(2)}) collective-permute-start(bf16[8,256,128]{2,1,0:T(8,128)(2,1)S(1)} %collective-permute-done.10.refs_2_), channel_id=1, source_target_pairs={{0,1},{1,0},{2,3},{3,2},{4,5},{5,4},{6,7},{7,6},{8,9},{9,8},{10,11... | collective-permute-start | bytes 1572872 | tf_op jit(solution)/shard_map/ppermute | solution.py:270

commit v2 on v1

--- a/solution.py
+++ b/solution.py
@@ -301,7 +301,8 @@
     return lax.optimization_barrier(tuple(values) + tuple(others))[: len(values)]
 
 
-def join(held, more):
+def join(held, more, others=()):
+    (held,) = after([held], others)
     (room,) = after([jnp.concatenate([held, held])], ())
     return lax.dynamic_update_slice(room, more, (held.shape[0], 0, 0))
 
@@ -322,12 +323,10 @@
 
 def gather_two(first, second, dims):
     first_far = swap(first, dims, 0, 2)
-    (room,) = after([jnp.concatenate([first, first])], ())
-    (second,) = after([second], [room])
     other = swap_times(second, 1, 2)
     pair = join(second, other)
     pair_far = swap(pair, dims, 0, 2)
-    (first_two,) = after([lax.dynamic_update_slice(room, first_far, (1, 0, 0))], [pair])
+    (first_two,) = after([join(first, first_far, [pair])], [pair])
     first_near = swap(first_two, dims, 0, 1)
     pair_two = jnp.concatenate([pair, pair_far])
     (first_near,) = after([first_near], [pair_two])
@@ -378,7 +377,7 @@
     blocks = [own[None] for own in white]
     if paired:
         *gathered, near = gather_two(*blocks, dims)
-        (tiles,) = after([tiles], [near])
+        tiles, counts = after([tiles, counts], [near])
     else:
         gathered = [gather_one(own, dims) for own in blocks]
 

time: 50.6 us -> 48.5 us (0.958); the launches traced: 50 us -> 48.4 us
  waiting for transfers between devices: 18.2 us -> 15.9 us
  starting transfers between devices: 13 us -> 13.7 us
    ppermute x1, starting transfers between devices: 1.56 us -> 3 us  [swap_times(): lax.ppermute(value, 'tm', [((t + step) % times, t) for t in range(times)])]
    ppermute x1, waiting for transfers between devices: 1.4 us -> 0.01 us  [swap_times(): lax.ppermute(value, 'tm', [((t + step) % times, t) for t in range(times)])]
    concatenate x1 -> x2, other arithmetic: 0.91 us -> 1.86 us  [join(): room, = after([jnp.concatenate([held, held])], ())]
    concatenate x1 -> x0, other arithmetic: 0.92 us -> none  [gather_two(): room, = after([jnp.concatenate([first, first])], ())]
    ppermute x1, starting transfers between devices: 1.56 us -> 0.71 us  [shards(): arrived[step] = lax.ppermute(arrived[step], 'tm', moves)]
    ppermute x10, waiting for transfers between devices: 14.8 us -> 14.3 us  [swap(): return lax.ppermute(value, 'pair', moves)]
  transfers between devices with their start and end apart: 12 -> 12, of which waited for: 6 -> 7; matrix products, arithmetic and copies ran while one was open for 9% -> 9% of each run, Pallas kernels for 7% -> 8%
where the time goes in v2:
time: 48.5 us; the launch traced here: 48.4 us
  waiting for transfers between devices  15.9 us (33%)
  starting transfers between devices  13.7 us (28%)
  Pallas kernels  13.6 us (28%)
  other arithmetic  3.51 us (7%)
  local copies, waits for them, and re-layouts  0.91 us (2%)
  between operations  0.77 us (2%)
    ppermute x10, waiting for transfers between devices, swap(): return lax.ppermute(value, 'pair', moves)  14.3 us
    ppermute x10, starting transfers between devices, swap(): return lax.ppermute(value, 'pair', moves)  9.95 us
    pallas_call x1, Pallas kernels, shards(): pl.pallas_call(functools.partial(stack_kernel, bins, rows, times, chunk,...  6.75 us
    pallas_call x1, Pallas kernels, shards(): pl.pallas_call(functools.partial(whiten_kernel, bins), in_specs=[anywhere...  3.17 us
    ppermute x1, starting transfers between devices, swap_times(): lax.ppermute(value, 'tm', [((t + step) % times, t) for t in range(times)])  3 us
    pallas_call x1, Pallas kernels, shards(): pl.pallas_call(functools.partial(cross_kernel, bins, rows, chunk), in_spe...  2.77 us
    concatenate x2, other arithmetic, join(): room, = after([jnp.concatenate([held, held])], ())  1.86 us
    ppermute x1, waiting for transfers between devices, shards(): arrived[step] = lax.ppermute(arrived[step], 'tm', moves)  1.61 us
  transfers between devices with their start and end apart: 12, of which 7 were waited for; matrix products, arithmetic and copies ran while one was open for 9% of the time, Pallas kernels for 8%

profile of v2, /device:TPU:0, one launch (start us, length us, event | category | flops | bytes accessed | tf_op | source)
XLA Modules:
  0.0 48.4 jit_solution(18228282493891697287)
XLA Ops:
  0.0 3.2 %whiten.1 = (bf16[256,128]{1,0:T(8,128)(2,1)}, bf16[256,128]{1,0:T(8,128)(2,1)}) custom-call(f32[2,128,1024]{2,1,0:T(8,128)} %x_hbm.1, f32[256,1024]{1,0:T(8,128)} %constant.157.clone.table_hbm), custom_call_target="tpu_custom_call" | custom-call | tf_op jit(solution)/shard_map/whiten/pallas_call | solution.py:362
  3.2 3.0 %collective-permute-start = (bf16[1,256,128]{2,1,0:T(8,128)(2,1)}, bf16[1,256,128]{2,1,0:T(8,128)(2,1)S(1)}, u32[]{:S(2)}, u32[]{:S(2)}) collective-permute-start(bf16[1,256,128]{2,1,0:T(8,128)(2,1)} %bitcast.5), channel_id=1, source_target_pairs={{16,0},{0,16},{17,1},{1,17},{18,2},{2,18},{19,3},{3,19},{20,4},{4,... | collective-permute-start | bytes 196616 | tf_op jit(solution)/shard_map/ppermute | solution.py:311
  6.2 2.6 %collective-permute-start.1 = (bf16[1,256,128]{2,1,0:T(8,128)(2,1)}, bf16[1,256,128]{2,1,0:T(8,128)(2,1)S(1)}, u32[]{:S(2)}, u32[]{:S(2)}) collective-permute-start(bf16[1,256,128]{2,1,0:T(8,128)(2,1)} %bitcast.3), channel_id=1, source_target_pairs={{0,8},{1,9},{2,10},{3,11},{4,12},{5,13},{6,14},{7,15},{8,0},{9,1},... | collective-permute-start | bytes 196616 | tf_op jit(solution)/shard_map/ppermute | solution.py:270
  9.4 0.9 %pad_maximum_fusion.2 = bf16[2,256,128]{2,1,0:T(8,128)(2,1)S(1)} fusion(bf16[1,256,128]{2,1,0:T(8,128)(2,1)} %bitcast.6), kind=kLoop, calls=%fused_computation.10 | loop fusion | flops 65536 | bytes 196608 | tf_op jit(solution)/shard_map/concatenate | solution.py:306
  10.4 1.4 %collective-permute-start.3 = (bf16[2,256,128]{2,1,0:T(8,128)(2,1)S(1)}, bf16[2,256,128]{2,1,0:T(8,128)(2,1)S(1)}, u32[]{:S(2)}, u32[]{:S(2)}) collective-permute-start(bf16[2,256,128]{2,1,0:T(8,128)(2,1)S(1)} %constant_dynamic-update-slice_fusion.3), channel_id=1, source_target_pairs={{0,8},{1,9},{2,10},{3,11},{4,12},{5,13},{6,14},{7,15},{8,0},{9,1},... | collective-permute-start | bytes 393224 | tf_op jit(solution)/shard_map/ppermute | solution.py:270
  11.8 0.9 %pad_maximum_fusion.3 = bf16[2,256,128]{2,1,0:T(8,128)(2,1)S(1)} fusion(bf16[1,256,128]{2,1,0:T(8,128)(2,1)} %bitcast.4), kind=kLoop, calls=%fused_computation.11 | loop fusion | flops 65536 | bytes 196608 | tf_op jit(solution)/shard_map/concatenate | solution.py:306
  12.8 2.5 %collective-permute-start.2 = (bf16[2,256,128]{2,1,0:T(8,128)(2,1)S(1)}, bf16[2,256,128]{2,1,0:T(8,128)(2,1)S(1)}, u32[]{:S(2)}, u32[]{:S(2)}) collective-permute-start(bf16[2,256,128]{2,1,0:T(8,128)(2,1)S(1)} %constant_dynamic-update-slice_fusion.2), channel_id=1, source_target_pairs={{0,4},{1,5},{2,6},{3,7},{4,0},{5,1},{6,2},{7,3},{8,12},{9,13},{10,... | collective-permute-start | bytes 393224 | tf_op jit(solution)/shard_map/ppermute | solution.py:270
  15.3 0.8 %copy.8 = s32[3,2]{1,0:T(4,128)S(1)} copy(s32[3,2]{0,1:T(2,128)} %param.7) | data formatting | bytes 48 | tf_op jit(solution)/shard_map/optimization_barrier | solution.py:301
  16.2 0.8 %select_reduce_fusion = s32[6]{0:T(128)S(1)} fusion(s32[16]{0:T(128)} %param.6, s32[6]{0:T(128)S(1)} %eq.57), kind=kLoop, calls=%fused_computation.15 | loop fusion | flops 282 | bytes 112 | tf_op jit(solution)/shard_map/reduce_sum | solution.py:386
  17.0 2.0 %collective-permute-done.3 = bf16[2,256,128]{2,1,0:T(8,128)(2,1)S(1)} collective-permute-done((bf16[2,256,128]{2,1,0:T(8,128)(2,1)S(1)}, bf16[2,256,128]{2,1,0:T(8,128)(2,1)S(1)}, u32[]{:S(2)}, u32[]{:S(2)}) %collective-permute-start.3) | collective-permute-done | bytes 131104 | tf_op jit(solution)/shard_map/ppermute | solution.py:270
  19.0 0.2 collective-permute-start.8
  19.2 0.1 collective-permute-done.2
  19.3 1.6 %collective-permute-start.5 = (bf16[4,256,128]{2,1,0:T(8,128)(2,1)S(1)}, bf16[4,256,128]{2,1,0:T(8,128)(2,1)S(1)}, u32[]{:S(2)}, u32[]{:S(2)}) collective-permute-start(bf16[4,256,128]{2,1,0:T(8,128)(2,1)S(1)} %constant_dynamic-update-slice_fusion.refs_0_), channel_id=1, source_target_pairs={{0,2},{1,3},{2,0},{3,1},{4,6},{5,7},{6,4},{7,5},{8,10},{9,11},{10,... | collective-permute-start | bytes 786440 | tf_op jit(solution)/shard_map/ppermute | solution.py:270
  21.0 4.5 %collective-permute-done.8 = bf16[4,256,128]{2,1,0:T(8,128)(2,1)S(1)} collective-permute-done((bf16[4,256,128]{2,1,0:T(8,128)(2,1)S(1)}, bf16[4,256,128]{2,1,0:T(8,128)(2,1)S(1)}, u32[]{:S(2)}, u32[]{:S(2)}) %collective-permute-start.8) | collective-permute-done | bytes 262176 | tf_op jit(solution)/shard_map/ppermute | solution.py:270
  25.5 1.6 %collective-permute-start.10 = (bf16[8,256,128]{2,1,0:T(8,128)(2,1)S(1)}, bf16[8,256,128]{2,1,0:T(8,128)(2,1)S(1)}, u32[]{:S(2)}, u32[]{:S(2)}) collective-permute-start(bf16[8,256,128]{2,1,0:T(8,128)(2,1)S(1)} %pad_maximum_fusion.refs_0_), channel_id=1, source_target_pairs={{0,2},{1,3},{2,0},{3,1},{4,6},{5,7},{6,4},{7,5},{8,10},{9,11},{10,... | collective-permute-start | bytes 1572872 | tf_op jit(solution)/shard_map/ppermute | solution.py:270
  27.1 0.2 collective-permute-done.5.refs_2_
  27.3 1.4 %collective-permute-done.6.refs_3_ = bf16[4,256,128]{2,1,0:T(8,128)(2,1)S(1)} collective-permute-done((bf16[4,256,128]{2,1,0:T(8,128)(2,1)S(1)}, bf16[4,256,128]{2,1,0:T(8,128)(2,1)S(1)}, u32[]{:S(2)}, u32[]{:S(2)}) %collective-permute-start.6) | collective-permute-done | bytes 262176 | tf_op jit(solution)/shard_map/ppermute | solution.py:270
  28.8 1.0 %pick.1 = (bf16[3,384,128]{2,1,0:T(8,128)(2,1)S(1)}, bf16[3,384,128]{2,1,0:T(8,128)(2,1)S(1)}) custom-call(s32[14]{0:T(128)S(1)} %get-tuple-element.29.plan_ref, bf16[4,256,128]{2,1,0:T(8,128)(2,1)S(1)} %constant_dynamic-update-slice_fusion.refs_0_, bf16[4,256,128]{2,1,0:T(8,128)(2,1)S(1)} %collective-permute-done.4.refs_1_, ...), custom_call_target="tpu_custom_call" | custom-call | flops 1 | bytes 1 | tf_op jit(solution)/shard_map/pick/pallas_call | solution.py:406
  29.7 0.7 %collective-permute-start.7 = (bf16[3,384,128]{2,1,0:T(8,128)(2,1)S(1)}, bf16[3,384,128]{2,1,0:T(8,128)(2,1)S(1)}, u32[]{:S(2)}, u32[]{:S(2)}) collective-permute-start(bf16[3,384,128]{2,1,0:T(8,128)(2,1)S(1)} %get-tuple-element.23), channel_id=1, source_target_pairs={{0,16},{16,0},{1,17},{17,1},{2,18},{18,2},{3,19},{19,3},{4,20},{20... | collective-permute-start | bytes 884744 | tf_op jit(solution)/shard_map/ppermute | solution.py:422
  30.4 0.6 %multiply_convert_fusion.table_ref = bf16[128,256]{1,0:T(8,128)(2,1)S(1)} fusion(s32[256]{0:T(256)S(1)} %fusion.5, s32[128]{0:T(128)S(1)} %iota_add_fusion, pred[256]{0:T(512)(128)(4,1)S(1)} %fusion.10), kind=kLoop, calls=%fused_computation.12 | loop fusion | flops 589824 | bytes 67328 | tf_op jit(solution)/shard_map/convert_element_type | solution.py:33
  31.1 6.2 %collective-permute-done.10.refs_2_ = bf16[8,256,128]{2,1,0:T(8,128)(2,1)S(1)} collective-permute-done((bf16[8,256,128]{2,1,0:T(8,128)(2,1)S(1)}, bf16[8,256,128]{2,1,0:T(8,128)(2,1)S(1)}, u32[]{:S(2)}, u32[]{:S(2)}) %collective-permute-start.10) | collective-permute-done | bytes 524320 | tf_op jit(solution)/shard_map/ppermute | solution.py:270
  37.2 1.6 %collective-permute-done.7.refs_1_ = bf16[3,384,128]{2,1,0:T(8,128)(2,1)S(1)} collective-permute-done((bf16[3,384,128]{2,1,0:T(8,128)(2,1)S(1)}, bf16[3,384,128]{2,1,0:T(8,128)(2,1)S(1)}, u32[]{:S(2)}, u32[]{:S(2)}) %collective-permute-start.7) | collective-permute-done | bytes 294944 | tf_op jit(solution)/shard_map/ppermute | solution.py:422
  38.8 2.8 %cross.1.early_ref = bf16[3,32,128,256]{3,2,1,0:T(8,128)(2,1)S(1)} custom-call(s32[14]{0:T(128)S(1)} %get-tuple-element.29.plan_ref, bf16[3,384,128]{2,1,0:T(8,128)(2,1)S(1)} %get-tuple-element.25.refs_0_, bf16[3,384,128]{2,1,0:T(8,128)(2,1)S(1)} %collective-permute-done.7.refs_1_), custom_call_target="tpu_custom_call" | custom-call | tf_op jit(solution)/shard_map/cross/pallas_call | solution.py:424
  41.6 6.8 %stack.1 = f32[3,128,8192]{2,1,0:T(8,128)} custom-call(s32[14]{0:T(128)S(1)} %get-tuple-element.30.plan_ref, bf16[128,256]{1,0:T(8,128)(2,1)S(1)} %multiply_convert_fusion.table_ref, bf16[3,32,128,256]{3,2,1,0:T(8,128)(2,1)S(1)} %cross.1.early_ref, bf16[8,256,128]{2,1,0:T(8,128)(2,1)S(1)} %pad_maximum_fusion.refs_0_, ...), custom_call_target="tpu_custom_call" | custom-call | tf_op jit(solution)/shard_map/stack/pallas_call | solution.py:433
  (22 shorter events, 0.4 us)
Async XLA Ops:
  3.2 7.2 %collective-permute-start = (bf16[1,256,128]{2,1,0:T(8,128)(2,1)}, bf16[1,256,128]{2,1,0:T(8,128)(2,1)S(1)}, u32[]{:S(2)}, u32[]{:S(2)}) collective-permute-start(bf16[1,256,128]{2,1,0:T(8,128)(2,1)} %bitcast.5), channel_id=1, source_target_pairs={{16,0},{0,16},{17,1},{1,17},{18,2},{2,18},{19,3},{3,19},{20,4},{4,... | collective-permute-start | bytes 196616 | tf_op jit(solution)/shard_map/ppermute | solution.py:311
  6.2 6.6 %collective-permute-start.1 = (bf16[1,256,128]{2,1,0:T(8,128)(2,1)}, bf16[1,256,128]{2,1,0:T(8,128)(2,1)S(1)}, u32[]{:S(2)}, u32[]{:S(2)}) collective-permute-start(bf16[1,256,128]{2,1,0:T(8,128)(2,1)} %bitcast.3), channel_id=1, source_target_pairs={{0,8},{1,9},{2,10},{3,11},{4,12},{5,13},{6,14},{7,15},{8,0},{9,1},... | collective-permute-start | bytes 196616 | tf_op jit(solution)/shard_map/ppermute | solution.py:270
  10.4 8.6 %collective-permute-start.3 = (bf16[2,256,128]{2,1,0:T(8,128)(2,1)S(1)}, bf16[2,256,128]{2,1,0:T(8,128)(2,1)S(1)}, u32[]{:S(2)}, u32[]{:S(2)}) collective-permute-start(bf16[2,256,128]{2,1,0:T(8,128)(2,1)S(1)} %constant_dynamic-update-slice_fusion.3), channel_id=1, source_target_pairs={{0,8},{1,9},{2,10},{3,11},{4,12},{5,13},{6,14},{7,15},{8,0},{9,1},... | collective-permute-start | bytes 393224 | tf_op jit(solution)/shard_map/ppermute | solution.py:270
  12.8 6.5 %collective-permute-start.2 = (bf16[2,256,128]{2,1,0:T(8,128)(2,1)S(1)}, bf16[2,256,128]{2,1,0:T(8,128)(2,1)S(1)}, u32[]{:S(2)}, u32[]{:S(2)}) collective-permute-start(bf16[2,256,128]{2,1,0:T(8,128)(2,1)S(1)} %constant_dynamic-update-slice_fusion.2), channel_id=1, source_target_pairs={{0,4},{1,5},{2,6},{3,7},{4,0},{5,1},{6,2},{7,3},{8,12},{9,13},{10,... | collective-permute-start | bytes 393224 | tf_op jit(solution)/shard_map/ppermute | solution.py:270
  19.0 6.4 %collective-permute-start.8 = (bf16[4,256,128]{2,1,0:T(8,128)(2,1)S(1)}, bf16[4,256,128]{2,1,0:T(8,128)(2,1)S(1)}, u32[]{:S(2)}, u32[]{:S(2)}) collective-permute-start(bf16[4,256,128]{2,1,0:T(8,128)(2,1)S(1)} %pad_maximum_fusion.1), channel_id=1, source_target_pairs={{0,4},{1,5},{2,6},{3,7},{4,0},{5,1},{6,2},{7,3},{8,12},{9,13},{10,... | collective-permute-start | bytes 786440 | tf_op jit(solution)/shard_map/ppermute | solution.py:270
  19.3 7.9 %collective-permute-start.5 = (bf16[4,256,128]{2,1,0:T(8,128)(2,1)S(1)}, bf16[4,256,128]{2,1,0:T(8,128)(2,1)S(1)}, u32[]{:S(2)}, u32[]{:S(2)}) collective-permute-start(bf16[4,256,128]{2,1,0:T(8,128)(2,1)S(1)} %constant_dynamic-update-slice_fusion.refs_0_), channel_id=1, source_target_pairs={{0,2},{1,3},{2,0},{3,1},{4,6},{5,7},{6,4},{7,5},{8,10},{9,11},{10,... | collective-permute-start | bytes 786440 | tf_op jit(solution)/shard_map/ppermute | solution.py:270
  20.9 6.4 %collective-permute-start.4 = (bf16[4,256,128]{2,1,0:T(8,128)(2,1)S(1)}, bf16[4,256,128]{2,1,0:T(8,128)(2,1)S(1)}, u32[]{:S(2)}, u32[]{:S(2)}) collective-permute-start(bf16[4,256,128]{2,1,0:T(8,128)(2,1)S(1)} %constant_dynamic-update-slice_fusion.refs_0_), channel_id=1, source_target_pairs={{0,1},{1,0},{2,3},{3,2},{4,5},{5,4},{6,7},{7,6},{8,9},{9,8},{10,11... | collective-permute-start | bytes 786440 | tf_op jit(solution)/shard_map/ppermute | solution.py:270
  25.5 11.7 %collective-permute-start.10 = (bf16[8,256,128]{2,1,0:T(8,128)(2,1)S(1)}, bf16[8,256,128]{2,1,0:T(8,128)(2,1)S(1)}, u32[]{:S(2)}, u32[]{:S(2)}) collective-permute-start(bf16[8,256,128]{2,1,0:T(8,128)(2,1)S(1)} %pad_maximum_fusion.refs_0_), channel_id=1, source_target_pairs={{0,2},{1,3},{2,0},{3,1},{4,6},{5,7},{6,4},{7,5},{8,10},{9,11},{10,... | collective-permute-start | bytes 1572872 | tf_op jit(solution)/shard_map/ppermute | solution.py:270
  27.2 1.5 %collective-permute-start.6 = (bf16[4,256,128]{2,1,0:T(8,128)(2,1)S(1)}, bf16[4,256,128]{2,1,0:T(8,128)(2,1)S(1)}, u32[]{:S(2)}, u32[]{:S(2)}) collective-permute-start(bf16[4,256,128]{2,1,0:T(8,128)(2,1)S(1)} %collective-permute-done.5.refs_2_), channel_id=1, source_target_pairs={{0,1},{1,0},{2,3},{3,2},{4,5},{5,4},{6,7},{7,6},{8,9},{9,8},{10,11... | collective-permute-start | bytes 786440 | tf_op jit(solution)/shard_map/ppermute | solution.py:270
  29.7 9.1 %collective-permute-start.7 = (bf16[3,384,128]{2,1,0:T(8,128)(2,1)S(1)}, bf16[3,384,128]{2,1,0:T(8,128)(2,1)S(1)}, u32[]{:S(2)}, u32[]{:S(2)}) collective-permute-start(bf16[3,384,128]{2,1,0:T(8,128)(2,1)S(1)} %get-tuple-element.23), channel_id=1, source_target_pairs={{0,16},{16,0},{1,17},{17,1},{2,18},{18,2},{3,19},{19,3},{4,20},{20... | collective-permute-start | bytes 884744 | tf_op jit(solution)/shard_map/ppermute | solution.py:422
  30.4 11.2 %collective-permute-start.9 = (bf16[8,256,128]{2,1,0:T(8,128)(2,1)S(1)}, bf16[8,256,128]{2,1,0:T(8,128)(2,1)S(1)}, u32[]{:S(2)}, u32[]{:S(2)}) collective-permute-start(bf16[8,256,128]{2,1,0:T(8,128)(2,1)S(1)} %pad_maximum_fusion.refs_0_), channel_id=1, source_target_pairs={{0,1},{1,0},{2,3},{3,2},{4,5},{5,4},{6,7},{7,6},{8,9},{9,8},{10,11... | collective-permute-start | bytes 1572872 | tf_op jit(solution)/shard_map/ppermute | solution.py:270
  38.8 2.8 %collective-permute-start.11 = (bf16[8,256,128]{2,1,0:T(8,128)(2,1)S(1)}, bf16[8,256,128]{2,1,0:T(8,128)(2,1)S(1)}, u32[]{:S(2)}, u32[]{:S(2)}) collective-permute-start(bf16[8,256,128]{2,1,0:T(8,128)(2,1)S(1)} %collective-permute-done.10.refs_2_), channel_id=1, source_target_pairs={{0,1},{1,0},{2,3},{3,2},{4,5},{5,4},{6,7},{7,6},{8,9},{9,8},{10,11... | collective-permute-start | bytes 1572872 | tf_op jit(solution)/shard_map/ppermute | solution.py:270
